TPU v7x, 32 devices: a whole 2x2x4 slice. The times are simulated.
32 devices in a mesh: grp: 8 (over y, x, core), dev: 4 (over z).
Axes of the slice: x: 2, y: 2, z: 4, core: 2. Of those that a mesh axis runs over, the one named last changes fastest.
Arguments:
- images: float32 [2048, 1152], P(('grp', 'dev')), may hold values from -0.2 to 0.2
- texts: float32 [2048, 1152], P(('grp', 'dev')), may hold values from -0.2 to 0.2
- log_temp: float32 [1], replicated, may hold values from 1.6 to 3
- bias: float32 [1], replicated, may hold values from -3 to -1
Outputs:
- grad_images: float32 [2048, 1152], P(('grp', 'dev'))
- grad_texts: float32 [2048, 1152], P(('grp', 'dev'))
All inputs are finite; a program needn't handle non-finite values.
Results may differ from a plain program's by a relative error of at most 0.0063.
Values may be sent and summed in bfloat16 or wider, within the bound.
A program may use at most 64 MiB of HBM per device.

v0:
```python
import jax
import jax.numpy as jnp
from jax import lax
from jax.sharding import PartitionSpec as P


def passed_along(block, axis, distance):
    devices = range(lax.axis_size(axis))
    route = [((i - distance) % len(devices), i) for i in devices]
    return lax.ppermute(block, axis, route)


def to_unit(raw):
    norm = jnp.sqrt(jnp.sum(raw * raw, axis=1, keepdims=True) + 1e-06)
    return (raw / norm, norm)


def from_unit(grad, unit, norm):
    return (grad - unit * jnp.sum(unit * grad, axis=1, keepdims=True)) / norm


def on_device(images, texts, log_temp, bias):
    temp = jnp.exp(log_temp[0])
    offset = bias[0]
    groups = lax.axis_size("grp")
    my_group = lax.axis_index("grp")
    my_member = lax.axis_index("dev")
    rows, width = images.shape
    img_unit, img_norm = to_unit(images)
    txt_unit, txt_norm = to_unit(texts)
    gathered = lax.all_gather(img_unit.astype(jnp.bfloat16), "dev", axis=0, tiled=True)
    pooled = gathered.shape[0]
    spans = ((0, rows, 1),)
    text_bf = txt_unit.astype(jnp.bfloat16)
    blocks = tuple((text_bf for start, count, _ in spans))
    columns = lax.broadcasted_iota(jnp.int32, (1, pooled), 1)

    def score(block, start, anchor):
        dots = lax.dot_general(
            block, gathered, (((1,), (1,)), ((), ())), preferred_element_type=jnp.float32
        )
        logits = temp * dots + offset
        diag_rows = (
            my_member * rows + start + lax.broadcasted_iota(jnp.int32, (block.shape[0], 1), 0)
        )
        hits = jnp.logical_and(diag_rows == columns, anchor == my_group)
        coeff = (jax.nn.sigmoid(logits) - hits.astype(jnp.float32)).astype(jnp.bfloat16)
        text_part = jnp.dot(coeff, gathered, preferred_element_type=jnp.float32)
        image_part = lax.dot_general(
            coeff, block, (((0,), (0,)), ((), ())), preferred_element_type=jnp.float32
        )
        return (text_part, image_part)

    def visit(step, blocks, grads, image_acc):
        for index, (start, count, direction) in enumerate(spans):
            anchor = jnp.mod(my_group - direction * step, groups)
            text_part, image_part = score(blocks[index], start, anchor)
            image_acc = image_acc + image_part
            grads = grads[:index] + (grads[index] + text_part,) + grads[index + 1 :]
        return (grads, image_acc)

    def advance(step, state):
        blocks, grads, image_acc = state
        grads, image_acc = visit(step, blocks, grads, image_acc)
        blocks = tuple(
            (passed_along(blocks[index], "grp", spans[index][2]) for index in range(len(spans)))
        )
        grads = tuple(
            (passed_along(grads[index], "grp", spans[index][2]) for index in range(len(spans)))
        )
        return (blocks, grads, image_acc)

    grads = tuple((jnp.zeros((count, width), jnp.float32) for _, count, _ in spans))
    image_acc = jnp.zeros((pooled, width), jnp.float32)
    blocks, grads, image_acc = lax.fori_loop(0, groups - 1, advance, (blocks, grads, image_acc))
    grads, image_acc = visit(groups - 1, blocks, grads, image_acc)
    homed = tuple(
        (passed_along(grads[index], "grp", spans[index][2]) for index in range(len(spans)))
    )
    text_sum = homed[0]
    image_sum = lax.psum_scatter(image_acc, "dev", scatter_dimension=0, tiled=True)
    grad_images = from_unit(temp * image_sum, img_unit, img_norm)
    grad_texts = from_unit(temp * text_sum, txt_unit, txt_norm)
    return (grad_images, grad_texts)


def solution(mesh):
    placed = (P(("grp", "dev"), None), P(("grp", "dev"), None), P(), P())
    return jax.shard_map(
        on_device,
        mesh=mesh,
        in_specs=placed,
        out_specs=(P(("grp", "dev"), None), P(("grp", "dev"), None)),
        check_vma=False,
    )
```

profile of v0, /device:TPU:0, one launch (start us, length us, event | category | flops | bytes accessed | tf_op | source)
XLA Modules:
  0.0 141.1 jit_solution(725885186403108135)
XLA Ops:
  7.2 1.1 multiply_reduce_fusion.3
  8.4 1.1 fusion.18
  10.1 1.1 multiply_reduce_fusion.2
  11.3 18.2 %all_gather.3 = bf16[256,1152]{1,0:T(8,128)(2,1)S(1)} all-gather(bf16[64,1152]{1,0:T(8,128)(2,1)S(1)} %fusion.19), channel_id=1, replica_groups=mesh['grp'=8,'dev'=4] {'dev'}, dimensions={0}, use_global_device_ids=true | all-gather | bytes 737280 | tf_op jit(solution)/shard_map/all_gather | solution.py:31
  30.2 69.6 %while.20 = (s32[]{:T(128)}, bf16[64,1152]{1,0:T(8,128)(2,1)S(1)}, f32[64,1152]{1,0:T(8,128)S(1)}, f32[256,1152]{1,0:T(8,128)S(1)}, f32[]{:T(128)}, /*index=5*/b...) while((s32[]{:T(128)}, bf16[64,1152]{1,0:T(8,128)(2,1)S(1)}, ...), condition=%wide.region_3.4_spmd.clone, body=%wide.region_2.3_spmd.clone.sunk | while | flops 114073680 | bytes 6587238 | solution.py:75
  30.3 1.0 fusion.45
  31.6 1.6 %collective-permute-start = (bf16[64,1152]{1,0:T(8,128)(2,1)S(1)}, bf16[64,1152]{1,0:T(8,128)(2,1)S(1)}, u32[]{:S(2)}, u32[]{:S(2)}) collective-permute-start(bf16[64,1152]{1,0:T(8,128)(2,1)S(1)} %copy.11), channel_id=1, source_target_pairs={{28,0},{0,4},{4,8},{8,12},{12,16},{16,20},{20,24},{24,28},{29,1},{... | collective-permute-start | bytes 442376 | tf_op jit(solution)/shard_map/while/body/eval_jaxpr/ppermute | solution.py:10
  33.7 6.5 %collective-permute-done = bf16[64,1152]{1,0:T(8,128)(2,1)S(1)} collective-permute-done((bf16[64,1152]{1,0:T(8,128)(2,1)S(1)}, bf16[64,1152]{1,0:T(8,128)(2,1)S(1)}, u32[]{:S(2)}, u32[]{:S(2)}) %collective-permute-start) | collective-permute-done | bytes 147488 | tf_op jit(solution)/shard_map/while/body/eval_jaxpr/ppermute | solution.py:10
  40.2 1.0 fusion.45
  42.7 7.4 %collective-permute-done = bf16[64,1152]{1,0:T(8,128)(2,1)S(1)} collective-permute-done((bf16[64,1152]{1,0:T(8,128)(2,1)S(1)}, bf16[64,1152]{1,0:T(8,128)(2,1)S(1)}, u32[]{:S(2)}, u32[]{:S(2)}) %collective-permute-start) | collective-permute-done | bytes 147488 | tf_op jit(solution)/shard_map/while/body/eval_jaxpr/ppermute | solution.py:10
  50.2 1.0 fusion.45
  52.0 8.0 %collective-permute-done = bf16[64,1152]{1,0:T(8,128)(2,1)S(1)} collective-permute-done((bf16[64,1152]{1,0:T(8,128)(2,1)S(1)}, bf16[64,1152]{1,0:T(8,128)(2,1)S(1)}, u32[]{:S(2)}, u32[]{:S(2)}) %collective-permute-start) | collective-permute-done | bytes 147488 | tf_op jit(solution)/shard_map/while/body/eval_jaxpr/ppermute | solution.py:10
  60.1 1.0 fusion.45
  62.0 8.0 %collective-permute-done = bf16[64,1152]{1,0:T(8,128)(2,1)S(1)} collective-permute-done((bf16[64,1152]{1,0:T(8,128)(2,1)S(1)}, bf16[64,1152]{1,0:T(8,128)(2,1)S(1)}, u32[]{:S(2)}, u32[]{:S(2)}) %collective-permute-start) | collective-permute-done | bytes 147488 | tf_op jit(solution)/shard_map/while/body/eval_jaxpr/ppermute | solution.py:10
  71.9 8.0 %collective-permute-done = bf16[64,1152]{1,0:T(8,128)(2,1)S(1)} collective-permute-done((bf16[64,1152]{1,0:T(8,128)(2,1)S(1)}, bf16[64,1152]{1,0:T(8,128)(2,1)S(1)}, u32[]{:S(2)}, u32[]{:S(2)}) %collective-permute-start) | collective-permute-done | bytes 147488 | tf_op jit(solution)/shard_map/while/body/eval_jaxpr/ppermute | solution.py:10
  80.0 1.0 fusion.45
  81.8 8.0 %collective-permute-done = bf16[64,1152]{1,0:T(8,128)(2,1)S(1)} collective-permute-done((bf16[64,1152]{1,0:T(8,128)(2,1)S(1)}, bf16[64,1152]{1,0:T(8,128)(2,1)S(1)}, u32[]{:S(2)}, u32[]{:S(2)}) %collective-permute-start) | collective-permute-done | bytes 147488 | tf_op jit(solution)/shard_map/while/body/eval_jaxpr/ppermute | solution.py:10
  89.9 1.0 fusion.45
  91.8 8.0 %collective-permute-done = bf16[64,1152]{1,0:T(8,128)(2,1)S(1)} collective-permute-done((bf16[64,1152]{1,0:T(8,128)(2,1)S(1)}, bf16[64,1152]{1,0:T(8,128)(2,1)S(1)}, u32[]{:S(2)}, u32[]{:S(2)}) %collective-permute-start) | collective-permute-done | bytes 147488 | tf_op jit(solution)/shard_map/while/body/eval_jaxpr/ppermute | solution.py:10
  100.1 1.4 convolution_add_fusion.2
  101.8 7.0 %collective-permute-done.2 = f32[64,1152]{1,0:T(8,128)S(1)} collective-permute-done((f32[64,1152]{1,0:T(8,128)S(1)}, f32[64,1152]{1,0:T(8,128)S(1)}, u32[]{:S(2)}, u32[]{:S(2)}) %collective-permute-start.2) | collective-permute-done | bytes 294944 | tf_op jit(solution)/shard_map/ppermute | solution.py:10
  109.9 21.4 %reduce-scatter.2.cloned.1.call-done = f32[64,1152]{1,0:T(8,128)} async-done(((f32[256,1152]{1,0:T(8,128)}), f32[64,1152]{1,0:T(8,128)}) %reduce-scatter.2.cloned.1.call-update) | async-done | bytes 294928 | tf_op jit(solution)/shard_map/reduce_scatter | solution.py:81
  131.3 1.2 multiply_reduce_fusion.1
  132.4 1.8 %subtract_divide_fusion.1 = f32[64,1152]{1,0:T(8,128)} fusion(f32[64,1152]{1,0:T(8,128)} %reduce-scatter.2.cloned.1.call-done, f32[64]{0:T(128)S(1)} %multiply_reduce_fusion.1, f32[64]{0:T(128)S(1)} %add_sqrt_fusion, f32[]{:T(128)} %bitcast, f32[64,1152]{1,0:T(8,128)S(1)} %copy-done.1), kind=kLoop, calls=%fused_computation.26 | loop fusion | flops 368640 | bytes 885252 | tf_op jit(solution)/shard_map/div | solution.py:19
  (66 shorter events, 9.5 us)
Async XLA Ops:
  7.2 4.1 %copy-start.1 = (f32[64,1152]{1,0:T(8,128)S(1)}, f32[64,1152]{1,0:T(8,128)}, u32[]{:S(2)}) copy-start(f32[64,1152]{1,0:T(8,128)} %param.6) | copy-start | bytes 884740
  7.2 124.1 %reduce-scatter.2.cloned.1.call-start = ((), (), s32[]{:S(2)}) async-start(), calls=%async_computation.1 | async-start | bytes 1474560 | tf_op jit(solution)/shard_map/reduce_scatter | solution.py:81
  31.5 8.7 %collective-permute-start.1 = (f32[64,1152]{1,0:T(8,128)S(1)}, f32[64,1152]{1,0:T(8,128)S(1)}, u32[]{:S(2)}, u32[]{:S(2)}) collective-permute-start(f32[64,1152]{1,0:T(8,128)S(1)} %convolution_add_fusion.6), channel_id=1, source_target_pairs={{28,0},{0,4},{4,8},{8,12},{12,16},{16,20},{20,24},{24,28},{29,1},{... | collective-permute-start | bytes 884744 | tf_op jit(solution)/shard_map/while/body/eval_jaxpr/ppermute | solution.py:10
  31.6 8.6 %collective-permute-start = (bf16[64,1152]{1,0:T(8,128)(2,1)S(1)}, bf16[64,1152]{1,0:T(8,128)(2,1)S(1)}, u32[]{:S(2)}, u32[]{:S(2)}) collective-permute-start(bf16[64,1152]{1,0:T(8,128)(2,1)S(1)} %copy.11), channel_id=1, source_target_pairs={{28,0},{0,4},{4,8},{8,12},{12,16},{16,20},{20,24},{24,28},{29,1},{... | collective-permute-start | bytes 442376 | tf_op jit(solution)/shard_map/while/body/eval_jaxpr/ppermute | solution.py:10
  41.4 8.7 %collective-permute-start.1 = (f32[64,1152]{1,0:T(8,128)S(1)}, f32[64,1152]{1,0:T(8,128)S(1)}, u32[]{:S(2)}, u32[]{:S(2)}) collective-permute-start(f32[64,1152]{1,0:T(8,128)S(1)} %convolution_add_fusion.6), channel_id=1, source_target_pairs={{28,0},{0,4},{4,8},{8,12},{12,16},{16,20},{20,24},{24,28},{29,1},{... | collective-permute-start | bytes 884744 | tf_op jit(solution)/shard_map/while/body/eval_jaxpr/ppermute | solution.py:10
  41.5 8.6 %collective-permute-start = (bf16[64,1152]{1,0:T(8,128)(2,1)S(1)}, bf16[64,1152]{1,0:T(8,128)(2,1)S(1)}, u32[]{:S(2)}, u32[]{:S(2)}) collective-permute-start(bf16[64,1152]{1,0:T(8,128)(2,1)S(1)} %copy.11), channel_id=1, source_target_pairs={{28,0},{0,4},{4,8},{8,12},{12,16},{16,20},{20,24},{24,28},{29,1},{... | collective-permute-start | bytes 442376 | tf_op jit(solution)/shard_map/while/body/eval_jaxpr/ppermute | solution.py:10
  51.4 8.7 %collective-permute-start.1 = (f32[64,1152]{1,0:T(8,128)S(1)}, f32[64,1152]{1,0:T(8,128)S(1)}, u32[]{:S(2)}, u32[]{:S(2)}) collective-permute-start(f32[64,1152]{1,0:T(8,128)S(1)} %convolution_add_fusion.6), channel_id=1, source_target_pairs={{28,0},{0,4},{4,8},{8,12},{12,16},{16,20},{20,24},{24,28},{29,1},{... | collective-permute-start | bytes 884744 | tf_op jit(solution)/shard_map/while/body/eval_jaxpr/ppermute | solution.py:10
  51.4 8.6 %collective-permute-start = (bf16[64,1152]{1,0:T(8,128)(2,1)S(1)}, bf16[64,1152]{1,0:T(8,128)(2,1)S(1)}, u32[]{:S(2)}, u32[]{:S(2)}) collective-permute-start(bf16[64,1152]{1,0:T(8,128)(2,1)S(1)} %copy.11), channel_id=1, source_target_pairs={{28,0},{0,4},{4,8},{8,12},{12,16},{16,20},{20,24},{24,28},{29,1},{... | collective-permute-start | bytes 442376 | tf_op jit(solution)/shard_map/while/body/eval_jaxpr/ppermute | solution.py:10
  61.3 8.7 %collective-permute-start.1 = (f32[64,1152]{1,0:T(8,128)S(1)}, f32[64,1152]{1,0:T(8,128)S(1)}, u32[]{:S(2)}, u32[]{:S(2)}) collective-permute-start(f32[64,1152]{1,0:T(8,128)S(1)} %convolution_add_fusion.6), channel_id=1, source_target_pairs={{28,0},{0,4},{4,8},{8,12},{12,16},{16,20},{20,24},{24,28},{29,1},{... | collective-permute-start | bytes 884744 | tf_op jit(solution)/shard_map/while/body/eval_jaxpr/ppermute | solution.py:10
  61.4 8.6 %collective-permute-start = (bf16[64,1152]{1,0:T(8,128)(2,1)S(1)}, bf16[64,1152]{1,0:T(8,128)(2,1)S(1)}, u32[]{:S(2)}, u32[]{:S(2)}) collective-permute-start(bf16[64,1152]{1,0:T(8,128)(2,1)S(1)} %copy.11), channel_id=1, source_target_pairs={{28,0},{0,4},{4,8},{8,12},{12,16},{16,20},{20,24},{24,28},{29,1},{... | collective-permute-start | bytes 442376 | tf_op jit(solution)/shard_map/while/body/eval_jaxpr/ppermute | solution.py:10
  71.2 8.7 %collective-permute-start.1 = (f32[64,1152]{1,0:T(8,128)S(1)}, f32[64,1152]{1,0:T(8,128)S(1)}, u32[]{:S(2)}, u32[]{:S(2)}) collective-permute-start(f32[64,1152]{1,0:T(8,128)S(1)} %convolution_add_fusion.6), channel_id=1, source_target_pairs={{28,0},{0,4},{4,8},{8,12},{12,16},{16,20},{20,24},{24,28},{29,1},{... | collective-permute-start | bytes 884744 | tf_op jit(solution)/shard_map/while/body/eval_jaxpr/ppermute | solution.py:10
  71.3 8.6 %collective-permute-start = (bf16[64,1152]{1,0:T(8,128)(2,1)S(1)}, bf16[64,1152]{1,0:T(8,128)(2,1)S(1)}, u32[]{:S(2)}, u32[]{:S(2)}) collective-permute-start(bf16[64,1152]{1,0:T(8,128)(2,1)S(1)} %copy.11), channel_id=1, source_target_pairs={{28,0},{0,4},{4,8},{8,12},{12,16},{16,20},{20,24},{24,28},{29,1},{... | collective-permute-start | bytes 442376 | tf_op jit(solution)/shard_map/while/body/eval_jaxpr/ppermute | solution.py:10
  81.2 8.7 %collective-permute-start.1 = (f32[64,1152]{1,0:T(8,128)S(1)}, f32[64,1152]{1,0:T(8,128)S(1)}, u32[]{:S(2)}, u32[]{:S(2)}) collective-permute-start(f32[64,1152]{1,0:T(8,128)S(1)} %convolution_add_fusion.6), channel_id=1, source_target_pairs={{28,0},{0,4},{4,8},{8,12},{12,16},{16,20},{20,24},{24,28},{29,1},{... | collective-permute-start | bytes 884744 | tf_op jit(solution)/shard_map/while/body/eval_jaxpr/ppermute | solution.py:10
  81.2 8.6 %collective-permute-start = (bf16[64,1152]{1,0:T(8,128)(2,1)S(1)}, bf16[64,1152]{1,0:T(8,128)(2,1)S(1)}, u32[]{:S(2)}, u32[]{:S(2)}) collective-permute-start(bf16[64,1152]{1,0:T(8,128)(2,1)S(1)} %copy.11), channel_id=1, source_target_pairs={{28,0},{0,4},{4,8},{8,12},{12,16},{16,20},{20,24},{24,28},{29,1},{... | collective-permute-start | bytes 442376 | tf_op jit(solution)/shard_map/while/body/eval_jaxpr/ppermute | solution.py:10
  91.1 8.7 %collective-permute-start.1 = (f32[64,1152]{1,0:T(8,128)S(1)}, f32[64,1152]{1,0:T(8,128)S(1)}, u32[]{:S(2)}, u32[]{:S(2)}) collective-permute-start(f32[64,1152]{1,0:T(8,128)S(1)} %convolution_add_fusion.6), channel_id=1, source_target_pairs={{28,0},{0,4},{4,8},{8,12},{12,16},{16,20},{20,24},{24,28},{29,1},{... | collective-permute-start | bytes 884744 | tf_op jit(solution)/shard_map/while/body/eval_jaxpr/ppermute | solution.py:10
  91.2 8.6 %collective-permute-start = (bf16[64,1152]{1,0:T(8,128)(2,1)S(1)}, bf16[64,1152]{1,0:T(8,128)(2,1)S(1)}, u32[]{:S(2)}, u32[]{:S(2)}) collective-permute-start(bf16[64,1152]{1,0:T(8,128)(2,1)S(1)} %copy.11), channel_id=1, source_target_pairs={{28,0},{0,4},{4,8},{8,12},{12,16},{16,20},{20,24},{24,28},{29,1},{... | collective-permute-start | bytes 442376 | tf_op jit(solution)/shard_map/while/body/eval_jaxpr/ppermute | solution.py:10
  101.5 7.3 %copy-start = (f32[64,1152]{1,0:T(8,128)S(1)}, f32[64,1152]{1,0:T(8,128)}, u32[]{:S(2)}) copy-start(f32[64,1152]{1,0:T(8,128)} %param.7) | copy-start | bytes 884740
  101.7 7.1 %collective-permute-start.2 = (f32[64,1152]{1,0:T(8,128)S(1)}, f32[64,1152]{1,0:T(8,128)S(1)}, u32[]{:S(2)}, u32[]{:S(2)}) collective-permute-start(f32[64,1152]{1,0:T(8,128)S(1)} %convolution_add_fusion.3), channel_id=1, source_target_pairs={{28,0},{0,4},{4,8},{8,12},{12,16},{16,20},{20,24},{24,28},{29,1},{... | collective-permute-start | bytes 884744 | tf_op jit(solution)/shard_map/ppermute | solution.py:10
Sparse Core Ops, SparseCore 0:
  101.6 29.5 reduce-scatter.1
where the time goes:
time: 141 us
  waiting for transfers between devices  82.4 us (58%)
  blocking collectives  18.2 us (13%)
  between operations  15.5 us (11%)
  matrix products  14 us (10%)
  other arithmetic  7.4 us (5%)
  starting transfers between devices  3.06 us (2%)
    ppermute x15, waiting for transfers between devices, passed_along(): return lax.ppermute(block, axis, route)  61 us
    reduce_scatter x1, waiting for transfers between devices, on_device(): lax.psum_scatter(image_acc, 'dev', scatter_dimension=0, tiled=True)  21.4 us
    all_gather x1, blocking collectives, on_device(): lax.all_gather(img_unit.astype(jnp.bfloat16), 'dev', axis=0, tiled=True)  18.2 us
    dot_general x8, matrix products, score(): lax.dot_general(block, gathered, (((1,), (1,)), ((), ())), preferred_elem...  7.19 us
    dot_general x8, matrix products, score(): lax.dot_general(coeff, block, (((0,), (0,)), ((), ())), preferred_element...  5 us
    ppermute x15, starting transfers between devices, passed_along(): return lax.ppermute(block, axis, route)  3.02 us
  transfers between devices with their start and end apart: 16, of which 9 were waited for; matrix products, arithmetic and copies ran while one was open for 3% of the time, Pallas kernels for 0%

commit v1 on v0

v1 whole, which is shorter than its diff:
```python
import functools

import jax
import jax.numpy as jnp
from jax import lax
from jax.experimental import pallas as pl
from jax.experimental.pallas import tpu as pltpu
from jax.sharding import PartitionSpec as P

NT = (((1,), (1,)), ((), ()))
TN = (((0,), (0,)), ((), ()))


def dot(a, b, dims=(((1,), (0,)), ((), ()))):
    return lax.dot_general(a, b, dims, preferred_element_type=jnp.float32)


def to_unit(raw):
    norm = jnp.sqrt(jnp.sum(raw * raw, axis=1, keepdims=True) + 1e-06)
    return (raw / norm, norm)


def from_unit(grad, unit, norm):
    return (grad - unit * jnp.sum(unit * grad, axis=1, keepdims=True)) / norm


def flipped(index, mask):
    out, bit = index, 1
    while bit <= mask:
        if mask & bit:
            out = out + bit - 2 * bit * ((index // bit) % 2)
        bit *= 2
    return out


def kernel(
    groups, members,
    log_temp_ref, bias_ref, img_ref, txt_ref, grad_img_ref, grad_txt_ref,
    x, y, coeff, dx, dx_out, dx_in, dy_sib, dy_mine, dy_in, dy_out, dy_home,
    x_send, x_recv, y_send, y_recv, sib_send, sib_recv,
    dx_send, dx_recv, dys_send, dys_recv, dyo_send, dyo_recv,
):
    rows, width = img_ref.shape
    chips = groups // 2
    tree = members == 4
    grp = lax.axis_index("grp")
    me = lax.axis_index("dev")
    core = grp % 2
    chip = grp // 2
    sibling = {"grp": grp + 1 - 2 * core}

    def peer(k):
        return {"grp": 2 * flipped(chip, k) + core}

    def block(index):
        return pl.ds(pl.multiple_of(index * rows, rows), rows)

    def remote(src, dst, send, recv, device):
        return pltpu.make_async_remote_copy(
            src_ref=src, dst_ref=dst, send_sem=send, recv_sem=recv,
            device_id=device, device_id_type=pl.DeviceIdType.MESH,
        )

    barrier = pltpu.get_barrier_semaphore()
    for k in range(1, chips):
        pl.semaphore_signal(barrier, device_id=peer(k), device_id_type=pl.DeviceIdType.MESH)
    pl.semaphore_signal(barrier, device_id=sibling, device_id_type=pl.DeviceIdType.MESH)
    for k in range(1, members):
        pl.semaphore_signal(
            barrier, device_id={"dev": (me + k) % members}, device_id_type=pl.DeviceIdType.MESH
        )

    img_unit, img_norm = to_unit(img_ref[...])
    x[block(me), :] = img_unit.astype(jnp.bfloat16)
    txt_unit, txt_norm = to_unit(txt_ref[...])
    y[core, block(chip), :] = txt_unit.astype(jnp.bfloat16)
    temp = jnp.exp(jnp.full((1, 1), log_temp_ref[0], jnp.float32))
    offset = bias_ref[0]

    pl.semaphore_wait(barrier, chips + members - 1)

    side = me // 2
    pair = flipped(me, 1)
    across = 2 - side
    far = 3 - 3 * side
    inner = jnp.logical_or(me == 1, me == 2)

    def send_x(source, slot, device):
        held = x.at[block(source), :]
        return remote(held, held, x_send.at[slot], x_recv.at[source], {"dev": device})

    def send_y(k, owner):
        held = y.at[core, block(owner), :]
        return remote(held, held, y_send.at[k], y_recv.at[k], peer(k))

    def share_y(k, half):
        held = y.at[half, block(flipped(chip, k)), :]
        return remote(held, held, sib_send.at[k], sib_recv.at[k], sibling)

    if tree:
        own_x = [send_x(me, 0, pair), send_x(me, 1, across)]
    else:
        own_x = [send_x(me, k - 1, (me + k) % members) for k in range(1, members)]
    own_y = [send_y(k, chip) for k in range(1, chips)]
    for copy in own_x[:1] + own_y + own_x[1:]:
        copy.start()
    share_y(0, core).start()

    def relay(slot, source):
        @pl.when(inner)
        def _():
            send_x(source, 0, pair).wait_recv()
            send_x(source, slot, pair).start()

    for k in range(1, chips):
        if tree and k == chips - 1:
            relay(2, across)
        send_y(k, flipped(chip, k)).wait_recv()
        share_y(k, core).start()
    if tree:
        relay(3, far)
    for k in range(chips):
        share_y(k, 1 - core).wait_recv()

    row_ids = lax.broadcasted_iota(jnp.int32, (rows, chips * rows), 0)
    col_ids = lax.broadcasted_iota(jnp.int32, (rows, chips * rows), 1)
    diagonal = col_ids == row_ids + chip * rows

    def score(source):
        mine = x[block(source), :]
        total = None
        for half in range(2):
            texts = y[half]
            logits = temp * dot(mine, texts, NT) + offset
            own = jnp.logical_and(source == me, core == half)
            hits = jnp.where(jnp.logical_and(diagonal, own), 1.0, 0.0)
            part = (jax.nn.sigmoid(logits) - hits).astype(jnp.bfloat16)
            coeff[half, block(source), :] = part
            term = dot(part, texts)
            total = term if total is None else total + term
        dx[source] = total

    def await_x(source):
        send_x(source, 0, me).wait_recv()

    def send_dx(dest, device, slot, into):
        return remote(
            dx_out.at[dest], dx_in.at[into], dx_send.at[slot], dx_recv.at[into], {"dev": device}
        )

    def ship_dx(dest, device, slot, into, value):
        dx_out[dest] = value.astype(jnp.bfloat16)
        send_dx(dest, device, slot, into).start()

    if tree:
        @pl.when(jnp.logical_not(inner))
        def _():
            await_x(pair)
        @pl.when(inner)
        def _():
            await_x(pair)
        score(pair)
        ship_dx(pair, pair, 0, 0, dx[pair])

        @pl.when(jnp.logical_not(inner))
        def _():
            await_x(across)
            score(across)
            ship_dx(across, pair, 1, 2, dx[across])
            score(me)
            await_x(far)
            score(far)
            ship_dx(far, pair, 2, 3, dx[far])

        @pl.when(inner)
        def _():
            score(across)
            score(far)
            score(me)
    else:
        def direct(k, carry):
            source = (me + k) % members

            @pl.when(k > 0)
            def _():
                await_x(source)
            score(source)

            @pl.when(k > 0)
            def _():
                ship_dx(source, source, k - 1, k - 1, dx[source])
            return carry
        lax.fori_loop(0, members, direct, 0)

    def share_dy(k):
        held = block(flipped(chip, k))
        return remote(
            dy_sib.at[held, :], dy_in.at[held, :], dys_send.at[k], dys_recv.at[k], sibling
        )

    def send_dy(k):
        return remote(dy_out.at[k], dy_home.at[k], dyo_send.at[k], dyo_recv.at[k], peer(k))

    images = x[...]
    dy_sib[...] = dot(coeff[1 - core], images, TN).astype(jnp.bfloat16)
    order = list(range(chips - 1, -1, -1))
    for k in order:
        share_dy(k).start()
    dy_mine[...] = dot(coeff[core], images, TN)
    for k in order:
        share_dy(k).wait_recv()
        if k > 0:
            held = block(flipped(chip, k))
            summed = dy_mine[held, :] + dy_in[held, :].astype(jnp.float32)
            dy_out[k] = summed.astype(jnp.bfloat16)
            send_dy(k).start()

    if tree:
        @pl.when(inner)
        def _():
            for dest, into in ((across, 2), (far, 3)):
                send_dx(dest, dest, 0, into).wait_recv()
                ship_dx(dest, dest, into - 1, 1, dx[dest] + dx_in[into].astype(jnp.float32))

    total = dx[me]
    for into in range(2 if tree else members - 1):
        send_dx(me, me, 0, into).wait_recv()
        total = total + dx_in[into].astype(jnp.float32)
    grad_img_ref[...] = from_unit(temp * total, img_unit, img_norm)

    total = dy_mine[block(chip), :] + dy_in[block(chip), :].astype(jnp.float32)
    for k in range(1, chips):
        send_dy(k).wait_recv()
        total = total + dy_home[k].astype(jnp.float32)
    grad_txt_ref[...] = from_unit(temp * total, txt_unit, txt_norm)

    for copy in own_x + own_y:
        copy.wait_send()
    for k in range(chips):
        share_y(k, core).wait_send()
        share_dy(k).wait_send()
        if k > 0:
            send_dy(k).wait_send()
    if tree:
        for slot in range(3):
            send_dx(me, me, slot, 0).wait_send()

        @pl.when(inner)
        def _():
            send_x(across, 2, pair).wait_send()
            send_x(far, 3, pair).wait_send()
    else:
        for slot in range(members - 1):
            send_dx(me, me, slot, 0).wait_send()


def on_device(groups, members, images, texts, log_temp, bias):
    rows, width = images.shape
    chips = groups // 2
    half = chips * rows
    f32, bf16, dma = jnp.float32, jnp.bfloat16, pltpu.SemaphoreType.DMA
    vmem = pl.BlockSpec(memory_space=pltpu.VMEM)
    smem = pl.BlockSpec(memory_space=pltpu.SMEM)
    return pl.pallas_call(
        functools.partial(kernel, groups, members),
        out_shape=(jax.ShapeDtypeStruct((rows, width), f32),) * 2,
        in_specs=[smem, smem, vmem, vmem],
        out_specs=(vmem, vmem),
        scratch_shapes=[
            pltpu.VMEM((members * rows, width), bf16),
            pltpu.VMEM((2, half, width), bf16),
            pltpu.VMEM((2, members * rows, half), bf16),
            pltpu.VMEM((members, rows, width), f32),
            pltpu.VMEM((members, rows, width), bf16),
            pltpu.VMEM((max(members, 4), rows, width), bf16),
            pltpu.VMEM((half, width), bf16),
            pltpu.VMEM((half, width), f32),
            pltpu.VMEM((half, width), bf16),
            pltpu.VMEM((chips, rows, width), bf16),
            pltpu.VMEM((chips, rows, width), bf16),
            dma((max(members, 4),)), dma((members,)),
            dma((chips,)), dma((chips,)), dma((chips,)), dma((chips,)),
            dma((max(members, 4),)), dma((max(members, 4),)),
            dma((chips,)), dma((chips,)), dma((chips,)), dma((chips,)),
        ],
        compiler_params=pltpu.CompilerParams(
            collective_id=0, has_side_effects=True, vmem_limit_bytes=48 * 2**20
        ),
        cost_estimate=pl.CostEstimate(
            flops=12 * half * members * rows * width,
            bytes_accessed=16 * rows * width,
            transcendentals=2 * half * members * rows,
        ),
    )(log_temp, bias, images, texts)


def solution(mesh):
    placed = P(("grp", "dev"), None)
    return jax.shard_map(
        functools.partial(on_device, mesh.shape["grp"], mesh.shape["dev"]),
        mesh=mesh,
        in_specs=(placed, placed, P(), P()),
        out_specs=(placed, placed),
        check_vma=False,
    )
```

time: 141 us -> 38.6 us (0.27)
  waiting for transfers between devices: 82.4 us -> 0 us
  Pallas kernels: 0 us -> 33.1 us
  blocking collectives: 18.2 us -> 0 us
  matrix products: 14 us -> 0 us
  between operations: 15.5 us -> 1.94 us
  other arithmetic: 7.4 us -> 0 us
  local copies, waits for them, and re-layouts: 0.12 us -> 3.35 us
  starting transfers between devices: 3.06 us -> 0 us
    ppermute x15 -> x0, waiting for transfers between devices: 61 us -> none  [passed_along(): return lax.ppermute(block, axis, route)]
    pallas_call x0 -> x1, Pallas kernels: none -> 33.1 us  [on_device(): pl.pallas_call(functools.partial(kernel, groups, members), out_shape=(jax...]
    reduce_scatter x1 -> x0, waiting for transfers between devices: 21.4 us -> none  [on_device(): lax.psum_scatter(image_acc, 'dev', scatter_dimension=0, tiled=True)]
    all_gather x1 -> x0, blocking collectives: 18.2 us -> none  [on_device(): lax.all_gather(img_unit.astype(jnp.bfloat16), 'dev', axis=0, tiled=True)]
    dot_general x24 -> x0, matrix products: 14 us -> none  [the longest x8 7.19 us: score(): lax.dot_general(block, gathered, (((1,), (1,)), ((), ())), preferred_elem...]
    reduce_sum x4 -> x0, other arithmetic: 3.56 us -> none  [the longest x2 2.2 us: to_unit(): norm = jnp.sqrt(jnp.sum(raw * raw, axis=1, keepdims=True) + 1e-06)]
    unnamed x4 -> x6, local copies, waits for them, and re-layouts: 0.01 us -> 3.35 us
    ppermute x15 -> x0, starting transfers between devices: 3.02 us -> none  [passed_along(): return lax.ppermute(block, axis, route)]
  transfers between devices with their start and end apart: 16 -> 0, of which waited for: 9 -> 0; matrix products, arithmetic and copies ran while one was open for 3% -> 0% of each run, Pallas kernels for 0% -> 0%
where the time goes in v1:
time: 38.6 us; the launch traced here: 38.4 us
  Pallas kernels  33.1 us (86%)
  local copies, waits for them, and re-layouts  3.35 us (9%)
  between operations  1.94 us (5%)
    pallas_call x1, Pallas kernels, on_device(): pl.pallas_call(functools.partial(kernel, groups, members), out_shape=(jax...  33.1 us
    unnamed x6, local copies, waits for them, and re-layouts  3.35 us

profile of v1, /device:TPU:0, one launch (start us, length us, event | category | flops | bytes accessed | tf_op | source)
XLA Modules:
  0.0 38.4 jit_solution(12353156354683585186)
XLA Ops:
  1.9 0.0 copy-start
  1.9 1.0 %copy-done = f32[64,1152]{1,0:T(8,128)S(1)} copy-done((f32[64,1152]{1,0:T(8,128)S(1)}, f32[64,1152]{1,0:T(8,128)}, u32[]{:S(2)}) %copy-start) | copy-done | bytes 294936
  2.9 0.0 copy-start.1
  2.9 1.0 %copy-done.1 = f32[64,1152]{1,0:T(8,128)S(1)} copy-done((f32[64,1152]{1,0:T(8,128)S(1)}, f32[64,1152]{1,0:T(8,128)}, u32[]{:S(2)}) %copy-start.1) | copy-done | bytes 294936
  3.8 33.1 %shard_map.59 = (f32[64,1152]{1,0:T(8,128)S(1)}, f32[64,1152]{1,0:T(8,128)S(1)}) custom-call(f32[1]{0:T(128)S(6)} %copy.8.log_temp_ref, f32[1]{0:T(128)S(6)} %copy.9.bias_ref, f32[64,1152]{1,0:T(8,128)S(1)} %copy-done, f32[64,1152]{1,0:T(8,128)S(1)} %copy-done.1), custom_call_target="tpu_custom_call" | custom-call | flops 905969664 | bytes 1179648 | tf_op jit(solution)/shard_map/pallas_call | solution.py:264
  36.9 0.7 %copy.10 = f32[64,1152]{1,0:T(8,128)} copy(f32[64,1152]{1,0:T(8,128)S(1)} %get-tuple-element.4) | data formatting | bytes 589824
  37.7 0.7 %copy.11 = f32[64,1152]{1,0:T(8,128)} copy(f32[64,1152]{1,0:T(8,128)S(1)} %get-tuple-element.5) | data formatting | bytes 589824
Async XLA Ops:
  1.9 1.0 %copy-start = (f32[64,1152]{1,0:T(8,128)S(1)}, f32[64,1152]{1,0:T(8,128)}, u32[]{:S(2)}) copy-start(f32[64,1152]{1,0:T(8,128)} %img_ref.1) | copy-start | bytes 884740
  2.9 1.0 %copy-start.1 = (f32[64,1152]{1,0:T(8,128)S(1)}, f32[64,1152]{1,0:T(8,128)}, u32[]{:S(2)}) copy-start(f32[64,1152]{1,0:T(8,128)} %txt_ref.1) | copy-start | bytes 884740

commit v2 on v1

v2 whole, which is shorter than its diff:
```python
import functools

import jax
import jax.numpy as jnp
from jax import lax
from jax.experimental import pallas as pl
from jax.experimental.pallas import tpu as pltpu
from jax.sharding import PartitionSpec as P

PARTS = 2
NT = (((1,), (1,)), ((), ()))
TN = (((0,), (0,)), ((), ()))


def dot(a, b, dims=(((1,), (0,)), ((), ()))):
    return lax.dot_general(a, b, dims, preferred_element_type=jnp.float32)


def to_unit(raw):
    norm = jnp.sqrt(jnp.sum(raw * raw, axis=1, keepdims=True) + 1e-06)
    return (raw / norm, norm)


def from_unit(grad, unit, norm):
    return (grad - unit * jnp.sum(unit * grad, axis=1, keepdims=True)) / norm


def flipped(index, mask):
    out, bit = index, 1
    while bit <= mask:
        if mask & bit:
            out = out + bit - 2 * bit * ((index // bit) % 2)
        bit *= 2
    return out


def kernel(
    groups, members,
    log_temp_ref, bias_ref, img_hbm, txt_hbm, grad_img_ref, grad_txt_ref,
    img_ref, txt_ref, load_sem, x, y, coeff, dx, dx_out, dx_in, dy_sib, dy_mine, dy_in, dy_out, dy_home,
    x_send, x_recv, y_send, y_recv, sib_send, sib_recv,
    dx_send, dx_recv, dys_send, dys_recv, dyo_send, dyo_recv,
):
    rows, width = img_ref.shape
    chips = groups // 2
    tree = members == 4
    grp = lax.axis_index("grp")
    me = lax.axis_index("dev")
    core = grp % 2
    chip = grp // 2
    sibling = {"grp": grp + 1 - 2 * core}
    part = rows // PARTS
    load_img = pltpu.make_async_copy(img_hbm, img_ref, load_sem.at[0])
    load_txt = pltpu.make_async_copy(txt_hbm, txt_ref, load_sem.at[1])
    load_img.start()
    load_txt.start()

    def peer(k):
        return {"grp": 2 * flipped(chip, k) + core}

    def block(index):
        return pl.ds(pl.multiple_of(index * rows, rows), rows)

    def piece(index, c):
        return pl.ds(pl.multiple_of(index * rows + c * part, part), part)

    def remote(src, dst, send, recv, device):
        return pltpu.make_async_remote_copy(
            src_ref=src, dst_ref=dst, send_sem=send, recv_sem=recv,
            device_id=device, device_id_type=pl.DeviceIdType.MESH,
        )

    barrier = pltpu.get_barrier_semaphore()
    for k in range(1, chips):
        pl.semaphore_signal(barrier, device_id=peer(k), device_id_type=pl.DeviceIdType.MESH)
    pl.semaphore_signal(barrier, device_id=sibling, device_id_type=pl.DeviceIdType.MESH)
    for k in range(1, members):
        pl.semaphore_signal(
            barrier, device_id={"dev": (me + k) % members}, device_id_type=pl.DeviceIdType.MESH
        )

    load_img.wait()
    img_unit, img_norm = to_unit(img_ref[...])
    x[block(me), :] = img_unit.astype(jnp.bfloat16)
    load_txt.wait()
    txt_unit, txt_norm = to_unit(txt_ref[...])
    y[core, block(chip), :] = txt_unit.astype(jnp.bfloat16)
    temp = jnp.exp(jnp.full((1, 1), log_temp_ref[0], jnp.float32))
    offset = bias_ref[0]

    pl.semaphore_wait(barrier, chips + members - 1)

    side = me // 2
    pair = flipped(me, 1)
    across = 2 - side
    far = 3 - 3 * side
    inner = jnp.logical_or(me == 1, me == 2)

    def send_x(source, c, slot, device):
        held = x.at[piece(source, c), :]
        return remote(held, held, x_send.at[slot, c], x_recv.at[source, c], {"dev": device})

    def send_y(k, owner):
        held = y.at[core, block(owner), :]
        return remote(held, held, y_send.at[k], y_recv.at[k], peer(k))

    def share_y(k, half):
        held = y.at[half, block(flipped(chip, k)), :]
        return remote(held, held, sib_send.at[k], sib_recv.at[k], sibling)

    own_y = [send_y(k, chip) for k in range(1, chips)]
    if tree:
        own_x = [send_x(me, c, 0, pair) for c in range(PARTS)]
        for copy in own_x:
            copy.start()

        @pl.when(inner)
        def _():
            for c in range(PARTS):
                send_x(me, c, 1, across).start()
    else:
        own_x = [
            send_x(me, c, k - 1, (me + k) % members) for k in range(1, members) for c in range(PARTS)
        ]
        for copy in own_x:
            copy.start()
    for copy in own_y:
        copy.start()
    share_y(0, core).start()

    def relay_x(*steps):
        @pl.when(inner)
        def _():
            for source, c, slot, device in steps:
                send_x(source, c, 0, device).wait_recv()
                send_x(source, c, slot, device).start()

    def relay_y(k):
        send_y(k, flipped(chip, k)).wait_recv()
        share_y(k, core).start()

    if tree:
        for c in range(PARTS):
            relay_x((pair, c, 2, across), (across, c, 3, pair))
        relay_x((far, 0, 4, pair))
    for k in range(1, chips - 1):
        relay_y(k)
    if tree:
        relay_x(*((far, c, 4, pair) for c in range(1, PARTS)))
    relay_y(chips - 1)
    for k in range(chips):
        share_y(k, 1 - core).wait_recv()

    def score(first, count):
        extent = count * rows
        span = pl.ds(pl.multiple_of(first * rows, rows), extent)
        row_ids = lax.broadcasted_iota(jnp.int32, (extent, chips * rows), 0) + (first - me) * rows
        col_ids = lax.broadcasted_iota(jnp.int32, (extent, chips * rows), 1) - chip * rows
        mine = x[span, :]
        total = None
        for half in range(2):
            texts = y[half]
            logits = temp * dot(mine, texts, NT) + offset
            hits = (row_ids == col_ids) & (row_ids >= 0) & (row_ids < rows) & (core == half)
            coeffs = (jax.nn.sigmoid(logits) - jnp.where(hits, 1.0, 0.0)).astype(jnp.bfloat16)
            coeff[half, span, :] = coeffs
            term = dot(coeffs, texts)
            total = term if total is None else total + term
        dx[span, :] = total

    def await_x(source):
        for c in range(PARTS):
            send_x(source, c, 0, me).wait_recv()

    def send_dx(dest, c, device, slot, into):
        return remote(
            dx_out.at[piece(dest, c), :], dx_in.at[into, pl.ds(c * part, part), :],
            dx_send.at[slot, c], dx_recv.at[into, c], {"dev": device},
        )

    def ship_dx(dest, device, slot, into, c, value):
        dx_out[piece(dest, c), :] = value.astype(jnp.bfloat16)
        send_dx(dest, c, device, slot, into).start()

    def ship_own(dest, device, slot, into):
        for c in range(PARTS):
            ship_dx(dest, device, slot, into, c, dx[piece(dest, c), :])

    if tree:
        @pl.when(jnp.logical_not(inner))
        def _():
            await_x(pair)
            await_x(across)
            score(side, 3)
            ship_own(pair, pair, 0, 0)
            ship_own(across, pair, 1, 2)
            await_x(far)
            score(far, 1)
            ship_own(far, pair, 2, 3)

        @pl.when(inner)
        def _():
            score(0, 4)
            ship_own(pair, pair, 0, 0)
    else:
        def direct(k, carry):
            source = (me + k) % members

            @pl.when(k > 0)
            def _():
                await_x(source)
            score(source, 1)

            @pl.when(k > 0)
            def _():
                ship_own(source, source, k - 1, k - 1)
            return carry
        lax.fori_loop(0, members, direct, 0)

    def share_dy(k):
        held = block(flipped(chip, k))
        return remote(
            dy_sib.at[held, :], dy_in.at[held, :], dys_send.at[k], dys_recv.at[k], sibling
        )

    def send_dy(k):
        return remote(dy_out.at[k], dy_home.at[k], dyo_send.at[k], dyo_recv.at[k], peer(k))

    images = x[...]
    dy_sib[...] = dot(coeff[1 - core], images, TN).astype(jnp.bfloat16)
    order = list(range(chips - 1, -1, -1))
    for k in order:
        share_dy(k).start()
    dy_mine[...] = dot(coeff[core], images, TN)
    for k in order:
        share_dy(k).wait_recv()
        if k > 0:
            held = block(flipped(chip, k))
            summed = dy_mine[held, :] + dy_in[held, :].astype(jnp.float32)
            dy_out[k] = summed.astype(jnp.bfloat16)
            send_dy(k).start()

    if tree:
        @pl.when(inner)
        def _():
            for dest, into in ((across, 2), (far, 3)):
                for c in range(PARTS):
                    send_dx(dest, c, dest, 0, into).wait_recv()
                    passed = dx_in[into, pl.ds(c * part, part), :].astype(jnp.float32)
                    ship_dx(dest, dest, into - 1, 1, c, dx[piece(dest, c), :] + passed)

    total = dx[block(me), :]
    for into in range(2 if tree else members - 1):
        for c in range(PARTS):
            send_dx(me, c, me, 0, into).wait_recv()
        total = total + dx_in[into].astype(jnp.float32)
    grad_img_ref[...] = from_unit(temp * total, img_unit, img_norm)

    total = dy_mine[block(chip), :] + dy_in[block(chip), :].astype(jnp.float32)
    for k in range(1, chips):
        send_dy(k).wait_recv()
        total = total + dy_home[k].astype(jnp.float32)
    grad_txt_ref[...] = from_unit(temp * total, txt_unit, txt_norm)

    for copy in own_x + own_y:
        copy.wait_send()
    for k in range(chips):
        share_y(k, core).wait_send()
        share_dy(k).wait_send()
        if k > 0:
            send_dy(k).wait_send()
    for slot in range(3 if tree else members - 1):
        for c in range(PARTS):
            send_dx(me, c, me, slot, 0).wait_send()
    if tree:
        @pl.when(inner)
        def _():
            for c in range(PARTS):
                for slot in range(1, 5):
                    send_x(me, c, slot, pair).wait_send()


def on_device(groups, members, images, texts, log_temp, bias):
    rows, width = images.shape
    chips = groups // 2
    half = chips * rows
    f32, bf16, dma = jnp.float32, jnp.bfloat16, pltpu.SemaphoreType.DMA
    vmem = pl.BlockSpec(memory_space=pltpu.VMEM)
    hbm = pl.BlockSpec(memory_space=pltpu.HBM)
    smem = pl.BlockSpec(memory_space=pltpu.SMEM)
    return pl.pallas_call(
        functools.partial(kernel, groups, members),
        out_shape=(jax.ShapeDtypeStruct((rows, width), f32),) * 2,
        in_specs=[smem, smem, hbm, hbm],
        out_specs=(vmem, vmem),
        scratch_shapes=[
            pltpu.VMEM((rows, width), f32),
            pltpu.VMEM((rows, width), f32),
            dma((2,)),
            pltpu.VMEM((members * rows, width), bf16),
            pltpu.VMEM((2, half, width), bf16),
            pltpu.VMEM((2, members * rows, half), bf16),
            pltpu.VMEM((members * rows, width), f32),
            pltpu.VMEM((members * rows, width), bf16),
            pltpu.VMEM((max(members, 4), rows, width), bf16),
            pltpu.VMEM((half, width), bf16),
            pltpu.VMEM((half, width), f32),
            pltpu.VMEM((half, width), bf16),
            pltpu.VMEM((chips, rows, width), bf16),
            pltpu.VMEM((chips, rows, width), bf16),
            dma((max(members, 5), PARTS)), dma((members, PARTS)),
            dma((chips,)), dma((chips,)), dma((chips,)), dma((chips,)),
            dma((max(members, 4), PARTS)), dma((max(members, 4), PARTS)),
            dma((chips,)), dma((chips,)), dma((chips,)), dma((chips,)),
        ],
        compiler_params=pltpu.CompilerParams(
            collective_id=0, has_side_effects=True, vmem_limit_bytes=48 * 2**20
        ),
        cost_estimate=pl.CostEstimate(
            flops=12 * half * members * rows * width,
            bytes_accessed=16 * rows * width,
            transcendentals=2 * half * members * rows,
        ),
    )(log_temp, bias, images, texts)


def solution(mesh):
    placed = P(("grp", "dev"), None)
    return jax.shard_map(
        functools.partial(on_device, mesh.shape["grp"], mesh.shape["dev"]),
        mesh=mesh,
        in_specs=(placed, placed, P(), P()),
        out_specs=(placed, placed),
        check_vma=False,
    )
```

time: 38.6 us -> 37.7 us (0.977)
  Pallas kernels: 33.1 us -> 32.2 us
    pallas_call x1, Pallas kernels: 33.1 us -> 32.2 us  [on_device(): pl.pallas_call(functools.partial(kernel, groups, members), out_shape=(jax...]
where the time goes in v2:
time: 37.7 us; the launch traced here: 37.5 us
  Pallas kernels  32.2 us (85%)
  local copies, waits for them, and re-layouts  3.35 us (9%)
  between operations  1.94 us (5%)
    pallas_call x1, Pallas kernels, on_device(): pl.pallas_call(functools.partial(kernel, groups, members), out_shape=(jax...  32.2 us
    unnamed x6, local copies, waits for them, and re-layouts  3.35 us

profile of v2, /device:TPU:0, one launch (start us, length us, event | category | flops | bytes accessed | tf_op | source)
XLA Modules:
  0.0 37.5 jit_solution(15152355505171127853)
XLA Ops:
  1.9 0.0 copy-start
  1.9 1.0 %copy-done = f32[64,1152]{1,0:T(8,128)S(1)} copy-done((f32[64,1152]{1,0:T(8,128)S(1)}, f32[64,1152]{1,0:T(8,128)}, u32[]{:S(2)}) %copy-start) | copy-done | bytes 294936
  2.9 0.0 copy-start.1
  2.9 1.0 %copy-done.1 = f32[64,1152]{1,0:T(8,128)S(1)} copy-done((f32[64,1152]{1,0:T(8,128)S(1)}, f32[64,1152]{1,0:T(8,128)}, u32[]{:S(2)}) %copy-start.1) | copy-done | bytes 294936
  3.8 32.2 %shard_map.59 = (f32[64,1152]{1,0:T(8,128)S(1)}, f32[64,1152]{1,0:T(8,128)S(1)}) custom-call(f32[1]{0:T(128)S(6)} %copy.8.log_temp_ref, f32[1]{0:T(128)S(6)} %copy.9.bias_ref, f32[64,1152]{1,0:T(8,128)S(1)} %copy-done, f32[64,1152]{1,0:T(8,128)S(1)} %copy-done.1), custom_call_target="tpu_custom_call" | custom-call | flops 905969664 | bytes 1179648 | tf_op jit(solution)/shard_map/pallas_call | solution.py:291
  36.0 0.7 %copy.10 = f32[64,1152]{1,0:T(8,128)} copy(f32[64,1152]{1,0:T(8,128)S(1)} %get-tuple-element.4) | data formatting | bytes 589824
  36.8 0.7 %copy.11 = f32[64,1152]{1,0:T(8,128)} copy(f32[64,1152]{1,0:T(8,128)S(1)} %get-tuple-element.5) | data formatting | bytes 589824
Async XLA Ops:
  1.9 1.0 %copy-start = (f32[64,1152]{1,0:T(8,128)S(1)}, f32[64,1152]{1,0:T(8,128)}, u32[]{:S(2)}) copy-start(f32[64,1152]{1,0:T(8,128)} %img_hbm.1) | copy-start | bytes 884740
  2.9 1.0 %copy-start.1 = (f32[64,1152]{1,0:T(8,128)S(1)}, f32[64,1152]{1,0:T(8,128)}, u32[]{:S(2)}) copy-start(f32[64,1152]{1,0:T(8,128)} %txt_hbm.1) | copy-start | bytes 884740

commit v3 on v2

--- a/solution.py
+++ b/solution.py
@@ -314,7 +314,7 @@
             dma((chips,)), dma((chips,)), dma((chips,)), dma((chips,)),
         ],
         compiler_params=pltpu.CompilerParams(
-            collective_id=0, has_side_effects=True, vmem_limit_bytes=48 * 2**20
+            collective_id=0, has_side_effects=True, vmem_limit_bytes=54400 * 2**10
         ),
         cost_estimate=pl.CostEstimate(
             flops=12 * half * members * rows * width,

time: 37.7 us -> 36.4 us (0.966)
  local copies, waits for them, and re-layouts: 3.35 us -> 1.43 us
  Pallas kernels: 32.2 us -> 32.8 us
    unnamed x6 -> x2, local copies, waits for them, and re-layouts: 3.35 us -> 1.43 us
    pallas_call x1, Pallas kernels: 32.2 us -> 32.8 us  [on_device(): pl.pallas_call(functools.partial(kernel, groups, members), out_shape=(jax...]
where the time goes in v3:
time: 36.4 us; the launch traced here: 36.2 us
  Pallas kernels  32.8 us (90%)
  between operations  1.93 us (5%)
  local copies, waits for them, and re-layouts  1.43 us (4%)
    pallas_call x1, Pallas kernels, on_device(): pl.pallas_call(functools.partial(kernel, groups, members), out_shape=(jax...  32.8 us
    unnamed x2, local copies, waits for them, and re-layouts  1.43 us

profile of v3, /device:TPU:0, one launch (start us, length us, event | category | flops | bytes accessed | tf_op | source)
XLA Modules:
  0.0 36.2 jit_solution(5656481527003773817)
XLA Ops:
  1.9 32.8 %shard_map.59 = (f32[64,1152]{1,0:T(8,128)S(1)}, f32[64,1152]{1,0:T(8,128)S(1)}) custom-call(f32[1]{0:T(128)S(6)} %copy.8.log_temp_ref, f32[1]{0:T(128)S(6)} %copy.9.bias_ref, f32[64,1152]{1,0:T(8,128)} %img_hbm.1, f32[64,1152]{1,0:T(8,128)} %txt_hbm.1), custom_call_target="tpu_custom_call" | custom-call | flops 905969664 | bytes 1179648 | tf_op jit(solution)/shard_map/pallas_call | solution.py:291
  34.8 0.7 %copy.10 = f32[64,1152]{1,0:T(8,128)} copy(f32[64,1152]{1,0:T(8,128)S(1)} %get-tuple-element.4) | data formatting | bytes 589824
  35.5 0.7 %copy.11 = f32[64,1152]{1,0:T(8,128)} copy(f32[64,1152]{1,0:T(8,128)S(1)} %get-tuple-element.5) | data formatting | bytes 589824
